TPU v7x, 32 devices: a whole 2x2x4 slice. The times are simulated.
32 devices in a mesh: row: 4 (over y, x), col: 8 (over z, core).
Axes of the slice: x: 2, y: 2, z: 4, core: 2. Of those that a mesh axis runs over, the one named last changes fastest.
Arguments:
- front: float32 [16, 1024, 8, 2048], P(None, 'row', None, 'col'), may hold values from -6 to 6
- children: float32 [8, 4096, 4096], P('row', None, 'col'), may hold values from -6 to 6
- child_rows: int32 [8, 16], replicated, may hold values from 0 to 63, as said below
- owner_slots: int32 [8], replicated, may hold values from 0 to 1, as said below
- inverses: float32 [3, 256, 256], replicated, may hold values from -0.0390625 to 0.0390625
- pattern: int32 [64, 64], replicated, may hold values 0 or 1
Outputs:
- factored: float32 [16, 1024, 8, 2048], P(None, 'row', None, 'col')
Inputs may be any that keep to these rules, and one draw needn't show every extreme that they name: `child_rows`: the 16 entries of one slot are distinct. For each slot g there is an offset o_g such that entry k taken mod 8 equals (k // (16 / 8) + o_g) mod 8, and every offset 0 to 8 - 1 belongs to exactly 8 / 8 slots. Hence each residue mod 4 appears exactly 16 / 4 times in each slot. `owner_slots`: slots g = o * 2 + s belong to owner o; an owner's live slots come first, slot 0 of every owner is live, at least one owner has all 2 slots live and at least one other owner has fewer.
All inputs are finite; a program needn't handle non-finite values.
Results may differ from a plain program's by a relative error of at most 0.00014.
Values sent between devices are 32-bit elements; how exact they have to be, the bound alone decides.
A program may use at most 320 MiB of HBM per device.

v0:
```python
import jax
import jax.numpy as jnp
from jax import lax
from jax.sharding import PartitionSpec as P

precise = lax.Precision.HIGHEST


def from_root(block, axis, holder):
    block = jnp.where(lax.axis_index(axis) == holder, block, jnp.zeros_like(block))
    return lax.psum(block, axis)


def shards(front, children, child_rows, owner_slots, inverses, pattern):
    rows_n = lax.axis_size("row")
    cols_n = lax.axis_size("col")
    my_row = lax.axis_index("row")
    my_col = lax.axis_index("col")
    local_rows, tile_size, local_cols, _ = front.shape
    slots_here, child_order, child_width = children.shape
    kblocks = child_order // tile_size
    per_row = kblocks // rows_n
    per_col = child_width // tile_size
    slot_total = child_rows.shape[0]
    per_dest = slot_total // cols_n
    panel_count = inverses.shape[0]
    col_ratio = cols_n // rows_n
    position = jnp.arange(kblocks, dtype=jnp.int32)
    row_order = jnp.argsort(child_rows % rows_n * kblocks + position[None, :], axis=1)
    my_order = lax.dynamic_slice_in_dim(row_order, my_row * slots_here, slots_here, 0)
    my_rank = lax.dynamic_slice_in_dim(row_order, my_row * per_row, per_row, 1)
    row_blocks = jnp.take_along_axis(child_rows, my_rank, axis=1)
    col_blocks = child_rows.reshape(slot_total, cols_n, per_col)
    slot_ids = jnp.arange(slot_total, dtype=jnp.int32)
    local_row_ids = jnp.arange(local_rows, dtype=jnp.int32)
    local_col_ids = jnp.arange(local_cols, dtype=jnp.int32)
    blocks_in = children.reshape(slots_here, kblocks, tile_size, child_width)
    sorted_rows = jnp.take_along_axis(blocks_in, my_order[:, :, None, None], axis=1)
    outgoing = sorted_rows.reshape(slots_here, rows_n, per_row, tile_size, child_width)
    arrived = lax.all_to_all(outgoing, "row", split_axis=1, concat_axis=0, tiled=True)
    arrived = arrived.reshape(slot_total, per_row, tile_size, child_width)
    dest_by_src = jnp.transpose(col_blocks[:, :, 0] % cols_n)
    send_order = jnp.argsort(dest_by_src * slot_total + slot_ids[None, :], axis=1)
    my_send = lax.dynamic_index_in_dim(send_order, my_col, 0, keepdims=False)
    outgoing = jnp.take(arrived, my_send, axis=0).reshape(
        cols_n, per_dest, per_row, tile_size, child_width
    )
    landed = lax.all_to_all(outgoing, "col", split_axis=0, concat_axis=0, tiled=True)
    recv_slot = lax.dynamic_slice_in_dim(send_order, my_col * per_dest, per_dest, 1)
    got_rows = row_blocks[recv_slot]
    src_ids = jnp.arange(cols_n, dtype=jnp.int32)
    got_cols = col_blocks[recv_slot, src_ids[:, None]]
    live_flag = owner_slots[recv_slot].astype(jnp.float32)
    row_hits = ((got_rows // rows_n)[..., None] == local_row_ids).astype(jnp.float32)
    row_hits = row_hits * live_flag[:, :, None, None]
    col_hits = ((got_cols // cols_n)[..., None] == local_col_ids).astype(jnp.float32)
    pieces = landed.reshape(cols_n, per_dest, per_row, tile_size, per_col, tile_size)
    extend_sum = jnp.einsum("snpa,sntb,snpxty->axby", row_hits, col_hits, pieces, precision=precise)
    summed_front = front + extend_sum
    block_index = local_row_ids * rows_n + my_row
    col_index = local_col_ids * cols_n + my_col
    top_index = my_col // rows_n
    top_root = my_col % rows_n
    current = summed_front[:, :, 0, :]
    factors = []
    for step_index in range(panel_count):
        column = from_root(current, "col", step_index)
        factor = jnp.einsum("axy,zy->axz", column, inverses[step_index], precision=precise)
        factor = jnp.where(
            (block_index >= step_index)[:, None, None], factor, jnp.zeros_like(factor)
        )
        factors.append(factor)
        if step_index + 1 < panel_count:
            top_block = lax.dynamic_index_in_dim(factor, top_index, 0, keepdims=False)
            top_block = from_root(top_block, "row", top_root)
            reduced = current - jnp.einsum("axy,zy->axz", factor, top_block, precision=precise)
            current = jnp.where(my_col > step_index, reduced, current)
    lower = jnp.concatenate(factors, axis=2)
    lower_split = lower.reshape(local_cols, col_ratio, tile_size, panel_count * tile_size)
    chosen = lax.dynamic_index_in_dim(lower_split, top_index, 1, keepdims=False)
    across = from_root(chosen, "row", top_root)
    trailing_sum = jnp.einsum("axk,byk->axby", lower, across, precision=precise)
    block_mask = pattern.reshape(local_rows, rows_n, local_cols, cols_n)
    block_mask = lax.dynamic_index_in_dim(block_mask, my_row, 1, keepdims=False)
    block_mask = lax.dynamic_index_in_dim(block_mask, my_col, 2, keepdims=False)
    trailing = (
        (block_mask > 0)
        & (block_index >= panel_count)[:, None]
        & (col_index >= panel_count)[None, :]
    )
    result = jnp.where(trailing[:, None, :, None], summed_front - trailing_sum, summed_front)
    stacked = jnp.stack(factors, axis=0)
    mine_factor = lax.dynamic_index_in_dim(
        stacked, jnp.minimum(my_col, panel_count - 1), 0, keepdims=False
    )
    first_col = jnp.where(my_col < panel_count, mine_factor, result[:, :, 0, :])
    result = result.at[:, :, 0, :].set(first_col)
    return result


def solution(mesh):
    return jax.shard_map(
        shards,
        mesh=mesh,
        in_specs=(P(None, "row", None, "col"), P("row", None, "col"), P(), P(), P(), P()),
        out_specs=P(None, "row", None, "col"),
        check_vma=False,
    )
```

profile of v0, /device:TPU:0, one launch (start us, length us, event | category | flops | bytes accessed | tf_op | source)
XLA Modules:
  0.0 1667.9 jit_solution(10317902727512108828)
XLA Ops:
  8.5 14.7 gather_fusion.4
  23.1 7.7 broadcast_select_fusion
  30.9 7.5 copy.156
  38.4 7.0 all-to-all-start
  46.3 182.8 %all-to-all-done = f32[2,4,4,256,512]{4,3,2,0,1:T(8,128)} async-done(((f32[2,4,4,256,512]{4,3,2,0,1:T(8,128)}), f32[2,4,4,256,512]{4,3,2,0,1:T(8,128)}, u32[]{:S(2)}, u32[]{:S(2)}) %all-to-all-start) | async-done | bytes 16777248 | tf_op jit(solution)/shard_map/all_to_all | solution.py:40
  229.1 14.2 gather_fusion
  243.3 12.3 fusion.2
  255.6 5.9 all-to-all-start.1
  265.1 360.1 %all-to-all-done.1 = f32[8,1,4,256,512]{4,3,2,1,0:T(8,128)} async-done(((f32[8,1,4,256,512]{4,3,2,1,0:T(8,128)}), f32[8,1,4,256,512]{4,3,2,1,0:T(8,128)}, u32[]{:S(2)}, u32[]{:S(2)}) %all-to-all-start.1) | async-done | bytes 16777248 | tf_op jit(solution)/shard_map/all_to_all | solution.py:48
  625.2 17.4 %copy.158 = f32[8,1,4,256,512]{3,4,2,0,1:T(8,128)} copy(f32[8,1,4,256,512]{4,3,2,1,0:T(8,128)} %all-to-all-done.1) | data formatting | bytes 33554432 | tf_op jit(solution)/shard_map/all_to_all | solution.py:48
  642.5 19.8 %copy.162 = f32[8,4,256,2,256]{4,1,3,2,0:T(4,128)} copy(f32[8,4,256,2,256]{2,4,3,1,0:T(8,128)} %bitcast.125) | data formatting | bytes 33554432 | tf_op jit(solution)/shard_map/reshape.50
  662.4 59.5 %fusion.20 = f32[8,256,2,256,16]{3,4,2,1,0:T(8,128)} fusion(f32[8,4,256,2,256]{4,1,3,2,0:T(4,128)} %copy.162, f32[8]{0:T(128)S(1)} %convert_element_type.16, s32[8,4]{1,0:T(8,128)S(1)} %add_select_fusion.2), kind=kOutput, calls=%fused_computation.46 | convolution fusion | flops 805307392 | bytes 83886240 | tf_op jit(solution)/shard_map/snpa,sntb,snpxty->axby/dot_general | solution.py:58
  721.9 78.1 %bitcast_add_fusion = f32[16,256,8,256]{3,2,0,1:T(8,128)} fusion(f32[16,256,8,256]{3,2,1,0:T(8,128)} %param.8, f32[8,256,2,256,16]{3,4,2,1,0:T(8,128)} %fusion.20, s32[8,2]{0,1:T(2,128)S(1)} %copy.164), kind=kOutput, calls=%fused_computation.9 | convolution fusion | flops 1619001472 | bytes 134217792 | tf_op jit(solution)/shard_map/snpa,sntb,snpxty->axby/dot_general | solution.py:58
  799.9 12.2 slice.62
  816.7 94.5 %all-reduce.7.cloned.1.call-done = f32[16,256,256]{2,0,1:T(8,128)} async-done(((f32[16,256,256]{2,0,1:T(8,128)}), f32[16,256,256]{2,0,1:T(8,128)}) %all-reduce.7.cloned.1.call-update) | async-done | bytes 4194320 | tf_op jit(solution)/shard_map/psum | solution.py:11
  911.2 5.4 convolution_select_fusion.2
  920.1 42.7 %all-reduce.9.cloned.1.call-done = f32[256,256]{1,0:T(8,128)} async-done(((f32[256,256]{1,0:T(8,128)}), f32[256,256]{1,0:T(8,128)}) %all-reduce.9.cloned.1.call-update) | async-done | bytes 262160 | tf_op jit(solution)/shard_map/psum | solution.py:11
  962.8 10.3 broadcast_select_fusion.2
  973.2 96.6 %all-reduce.11.cloned.1.call-done = f32[16,256,256]{2,0,1:T(8,128)} async-done(((f32[16,256,256]{2,0,1:T(8,128)}), f32[16,256,256]{2,0,1:T(8,128)}) %all-reduce.11.cloned.1.call-update) | async-done | bytes 4194320 | tf_op jit(solution)/shard_map/psum | solution.py:11
  1078.3 43.1 %all-reduce.13.cloned.1.call-done = f32[256,256]{1,0:T(8,128)} async-done(((f32[256,256]{1,0:T(8,128)}), f32[256,256]{1,0:T(8,128)}) %all-reduce.13.cloned.1.call-update) | async-done | bytes 262160 | tf_op jit(solution)/shard_map/psum | solution.py:11
  1121.4 8.9 fusion.9
  1130.6 96.4 %all-reduce.15.cloned.1.call-done = f32[16,256,256]{2,0,1:T(8,128)} async-done(((f32[16,256,256]{2,0,1:T(8,128)}), f32[16,256,256]{2,0,1:T(8,128)}) %all-reduce.15.cloned.1.call-update) | async-done | bytes 4194320 | tf_op jit(solution)/shard_map/psum | solution.py:11
  1227.0 5.6 convolution_select_fusion
  1239.4 15.1 reshape.317
  1254.5 8.6 constant_dynamic-slice_fusion
  1269.5 5.9 fusion.11
  1275.3 131.5 %all-reduce.17.cloned.1.call-done = f32[8,256,768]{2,1,0:T(8,128)} async-done(((f32[8,256,768]{2,1,0:T(8,128)}), f32[8,256,768]{2,1,0:T(8,128)}) %all-reduce.17.cloned.1.call-update) | async-done | bytes 6291472 | tf_op jit(solution)/shard_map/psum | solution.py:11
  1406.8 86.7 %fusion.5 = f32[16,256,8,256]{3,0,2,1:T(8,128)} fusion(f32[8,256,768]{2,1,0:T(8,128)} %all-reduce.17.cloned.1.call-done, f32[16,256,256]{2,0,1:T(8,128)} %copy-done.7, f32[16,256,256]{2,0,1:T(8,128)} %copy-done.3, f32[16,256,256]{2,0,1:T(8,128)} %copy-done.5), kind=kOutput, calls=%fused_computation.16 | convolution fusion | flops 77315702784 | bytes 52428800 | tf_op jit(solution)/shard_map/axk,byk->axby/dot_general | solution.py:82
  1493.5 38.4 %subtract_select_fusion = f32[16,256,8,256]{3,2,0,1:T(8,128)} fusion(f32[16,256,8,256]{3,2,0,1:T(8,128)} %bitcast_add_fusion, f32[16,256,8,256]{3,0,2,1:T(8,128)} %fusion.5, pred[16,8]{1,0:T(8,128)(4,1)S(1)} %copy.148), kind=kLoop, calls=%fused_computation.8 | loop fusion | flops 16777216 | bytes 100663424 | tf_op jit(solution)/shard_map/jit(_where)/select_n | solution.py:91
  1531.9 15.2 broadcast_select_fusion.1
  1547.1 90.7 %scatter.4 = f32[16,256,8,256]{3,2,0,1:T(8,128)} dynamic-update-slice(f32[16,256,8,256]{3,2,0,1:T(8,128)} %subtract_select_fusion, f32[16,256,1,256]{3,2,0,1:T(1,128)} %broadcast_select_fusion.1, s32[]{:T(128)} %constant.195.clone.1, s32[]{:T(128)} %constant.195.clone.1, s32[]{:T(128)} %constant.195.clone.1, s32[]{:T(128)} %constant.195.clone.1) | dynamic-update-slice | bytes 8388612 | tf_op jit(solution)/shard_map/scatter | solution.py:97
  1637.8 22.9 %copy.178 = f32[16,256,8,256]{3,2,1,0:T(8,128)} copy(f32[16,256,8,256]{3,2,0,1:T(8,128)} %scatter.4) | data formatting | bytes 67108864 | tf_op jit(solution)/shard_map/scatter | solution.py:97
  (94 shorter events, 36.3 us)
Async XLA Ops:
  6.5 255.4 %copy-start = (s32[8]{0:T(128)S(1)}, s32[8]{0:T(128)}, u32[]{:S(2)}) copy-start(s32[8]{0:T(128)} %param.11) | copy-start | bytes 100
  38.4 190.7 %all-to-all-start = ((f32[2,4,4,256,512]{4,3,2,0,1:T(8,128)}), f32[2,4,4,256,512]{4,3,2,0,1:T(8,128)}, u32[]{:S(2)}, u32[]{:S(2)}) async-start(f32[2,4,4,256,512]{4,3,2,0,1:T(8,128)} %copy.156), calls=%async_computation | async-start | bytes 33554432 | tf_op jit(solution)/shard_map/all_to_all | solution.py:40
  255.6 7.4 copy-start.2
  255.6 369.6 %all-to-all-start.1 = ((f32[8,1,4,256,512]{4,3,2,1,0:T(8,128)}), f32[8,1,4,256,512]{4,3,2,1,0:T(8,128)}, u32[]{:S(2)}, u32[]{:S(2)}) async-start(f32[8,1,4,256,512]{4,3,2,1,0:T(8,128)} %fusion.2), calls=%async_computation.1 | async-start | bytes 33554432 | tf_op jit(solution)/shard_map/all_to_all | solution.py:48
  261.5 649.7 %all-reduce.7.cloned.1.call-start = ((), (), s32[]{:S(2)}) async-start(), calls=%async_computation.2 | async-start | bytes 8388608 | tf_op jit(solution)/shard_map/psum | solution.py:11
  812.2 1.9 copy-start.8
  816.6 94.6 %copy-start.9 = (f32[3,256,256]{2,1,0:T(8,128)S(1)}, f32[3,256,256]{2,1,0:T(8,128)}, u32[]{:S(2)}) copy-start(f32[3,256,256]{2,1,0:T(8,128)} %param.12) | copy-start | bytes 2359300
  816.6 146.2 %all-reduce.9.cloned.1.call-start = ((), (), s32[]{:S(2)}) async-start(), calls=%async_computation.3 | async-start | bytes 524288 | tf_op jit(solution)/shard_map/psum | solution.py:11
  916.6 2.0 copy-start.5
  919.6 150.1 %all-reduce.11.cloned.1.call-start = ((), (), s32[]{:S(2)}) async-start(), calls=%async_computation.4 | async-start | bytes 8388608 | tf_op jit(solution)/shard_map/psum | solution.py:11
  973.1 148.3 %all-reduce.13.cloned.1.call-start = ((), (), s32[]{:S(2)}) async-start(), calls=%async_computation.5 | async-start | bytes 524288 | tf_op jit(solution)/shard_map/psum | solution.py:11
  1075.2 2.1 copy-start.3
  1078.3 148.7 %all-reduce.15.cloned.1.call-start = ((), (), s32[]{:S(2)}) async-start(), calls=%async_computation.6 | async-start | bytes 8388608 | tf_op jit(solution)/shard_map/psum | solution.py:11
  1130.4 276.5 %all-reduce.17.cloned.1.call-start = ((), (), s32[]{:S(2)}) async-start(), calls=%async_computation.7 | async-start | bytes 12582912 | tf_op jit(solution)/shard_map/psum | solution.py:11
  1227.0 7.5 copy-start.4
  1227.0 7.5 copy-start.6
  1232.6 1.9 copy-start.7
  1268.2 0.8 copy-start.10
  1637.8 22.9 %copy-start.1 = (s32[8]{0:T(128)S(1)}, s32[8]{0:T(128)}, u32[]{:S(2)}) copy-start(s32[8]{0:T(128)} %param.11) | copy-start | bytes 100
Sparse Core Ops, SparseCore 0:
  816.7 94.4 all-reduce.6
  919.8 42.9 all-reduce.8
  973.2 96.5 all-reduce.10
  1078.4 42.9 all-reduce.12
  1130.5 96.4 all-reduce.14
  1268.3 138.4 all-reduce.16
where the time goes:
time: 1680 us; the launch traced here: 1670 us
  waiting for transfers between devices  1050 us (62%)
  matrix products  260 us (15%)
  local copies, waits for them, and re-layouts  238 us (14%)
  other arithmetic  94.4 us (6%)
    psum x6, waiting for transfers between devices, from_root(): return lax.psum(block, axis)  505 us
    all_to_all x1, waiting for transfers between devices, shards(): lax.all_to_all(outgoing, 'col', split_axis=0, concat_axis=0, tiled=True)  360 us
    all_to_all x1, waiting for transfers between devices, shards(): lax.all_to_all(outgoing, 'row', split_axis=1, concat_axis=0, tiled=True)  183 us
    dot_general x2, matrix products, shards(): jnp.einsum('snpa,sntb,snpxty->axby', row_hits, col_hits, pieces, precisio...  138 us
    scatter x2, local copies, waits for them, and re-layouts, shards(): result = result.at[:, :, 0, :].set(first_col)  114 us
    dot_general x1, matrix products, shards(): trailing_sum = jnp.einsum('axk,byk->axby', lower, across, precision=precise)  86.7 us
    select_n x1, other arithmetic, shards(): jnp.where(trailing[:, None, :, None], summed_front - trailing_sum, summed...  38.4 us
  transfers between devices with their start and end apart: 8, of which 8 were waited for; matrix products, arithmetic and copies ran while one was open for 1% of the time, Pallas kernels for 0%

commit v1 on v0

--- a/solution.py
+++ b/solution.py
@@ -6,9 +6,15 @@
 precise = lax.Precision.HIGHEST
 
 
+def gather_and_add(value, mesh_axis):
+    parts = lax.all_gather(value, mesh_axis, axis=0, tiled=False)
+    result = parts.sum(axis=0)
+    return result
+
+
 def from_root(block, axis, holder):
     block = jnp.where(lax.axis_index(axis) == holder, block, jnp.zeros_like(block))
-    return lax.psum(block, axis)
+    return gather_and_add(block, axis)
 
 
 def shards(front, children, child_rows, owner_slots, inverses, pattern):

time: 1680 us -> 2400 us (1.43)
  waiting for transfers between devices: 1050 us -> 1670 us
  other arithmetic: 94.4 us -> 184 us
    all_gather x0 -> x6, waiting for transfers between devices: none -> 1130 us  [gather_and_add(): parts = lax.all_gather(value, mesh_axis, axis=0, tiled=False)]
    psum x6 -> x0, waiting for transfers between devices: 505 us -> none  [from_root(): return lax.psum(block, axis)]
    reduce_sum x0 -> x6, other arithmetic: none -> 69.3 us  [gather_and_add(): result = parts.sum(axis=0)]
  transfers between devices with their start and end apart: 8 -> 8, of which waited for: 8 -> 8; matrix products, arithmetic and copies ran while one was open for 1% -> 0% of each run, Pallas kernels for 0% -> 0%
where the time goes in v1:
time: 2400 us; the launch traced here: 2390 us
  waiting for transfers between devices  1670 us (70%)
  matrix products  261 us (11%)
  local copies, waits for them, and re-layouts  240 us (10%)
  other arithmetic  184 us (8%)
    all_gather x6, waiting for transfers between devices, gather_and_add(): parts = lax.all_gather(value, mesh_axis, axis=0, tiled=False)  1130 us
    all_to_all x1, waiting for transfers between devices, shards(): lax.all_to_all(outgoing, 'col', split_axis=0, concat_axis=0, tiled=True)  360 us
    all_to_all x1, waiting for transfers between devices, shards(): lax.all_to_all(outgoing, 'row', split_axis=1, concat_axis=0, tiled=True)  183 us
    dot_general x2, matrix products, shards(): jnp.einsum('snpa,sntb,snpxty->axby', row_hits, col_hits, pieces, precisio...  138 us
    scatter x2, local copies, waits for them, and re-layouts, shards(): result = result.at[:, :, 0, :].set(first_col)  114 us
    dot_general x1, matrix products, shards(): trailing_sum = jnp.einsum('axk,byk->axby', lower, across, precision=precise)  87.7 us
    reduce_sum x6, other arithmetic, gather_and_add(): result = parts.sum(axis=0)  69.3 us
  transfers between devices with their start and end apart: 8, of which 8 were waited for; matrix products, arithmetic and copies ran while one was open for 0% of the time, Pallas kernels for 0%

profile of v1, /device:TPU:0, one launch (start us, length us, event | category | flops | bytes accessed | tf_op | source)
XLA Modules:
  0.0 2388.1 jit_solution(16721462905899593699)
XLA Ops:
  8.5 14.7 gather_fusion.4
  23.1 7.7 broadcast_select_fusion.1
  30.9 7.5 copy.152
  46.3 182.8 %all-to-all-done = f32[2,4,4,256,512]{4,3,2,0,1:T(8,128)} async-done(((f32[2,4,4,256,512]{4,3,2,0,1:T(8,128)}), f32[2,4,4,256,512]{4,3,2,0,1:T(8,128)}, u32[]{:S(2)}, u32[]{:S(2)}) %all-to-all-start) | async-done | bytes 16777248 | tf_op jit(solution)/shard_map/all_to_all | solution.py:46
  229.1 14.2 gather_fusion
  243.3 12.3 fusion.2
  265.2 359.9 %all-to-all-done.1 = f32[8,1,4,256,512]{4,3,2,1,0:T(8,128)} async-done(((f32[8,1,4,256,512]{4,3,2,1,0:T(8,128)}), f32[8,1,4,256,512]{4,3,2,1,0:T(8,128)}, u32[]{:S(2)}, u32[]{:S(2)}) %all-to-all-start.1) | async-done | bytes 16777248 | tf_op jit(solution)/shard_map/all_to_all | solution.py:54
  625.2 17.4 copy.154
  642.5 19.8 copy.158
  662.4 59.5 %fusion.20 = f32[8,256,2,256,16]{3,4,2,1,0:T(8,128)} fusion(f32[8,4,256,2,256]{4,1,3,2,0:T(4,128)} %copy.158, f32[8]{0:T(128)S(1)} %convert_element_type.16, s32[8,4]{1,0:T(8,128)S(1)} %add_select_fusion.2), kind=kOutput, calls=%fused_computation.45 | convolution fusion | flops 805307392 | bytes 83886240 | tf_op jit(solution)/shard_map/snpa,sntb,snpxty->axby/dot_general | solution.py:64
  721.9 78.4 %bitcast_add_fusion = f32[16,256,8,256]{3,2,0,1:T(8,128)} fusion(f32[16,256,8,256]{3,2,1,0:T(8,128)} %param.8, f32[8,256,2,256,16]{3,4,2,1,0:T(8,128)} %fusion.20, s32[8,2]{0,1:T(2,128)S(1)} %copy.160), kind=kOutput, calls=%fused_computation.9 | convolution fusion | flops 1619001472 | bytes 134217792 | tf_op jit(solution)/shard_map/snpa,sntb,snpxty->axby/dot_general | solution.py:64
  800.2 17.7 broadcast_select_fusion.3
  818.0 286.6 %all-gather.15.cloned.1.call-done = f32[128,256,1,256]{3,2,0,1:T(1,128)} async-done(((f32[16,256,1,256]{3,2,0,1:T(1,128)}), f32[128,256,1,256]{3,2,0,1:T(1,128)}) %all-gather.15.cloned.1.call-update) | async-done | bytes 33554448 | tf_op jit(solution)/shard_map/all_gather | solution.py:10
  1104.6 25.1 %copy.198 = f32[128,256,1,256]{3,0,2,1:T(8,128)} copy(f32[128,256,1,256]{3,2,0,1:T(1,128)} %all-gather.15.cloned.1.call-done) | data formatting | bytes 67108864
  1129.8 15.2 reduce_sum.54
  1153.4 24.9 %all-gather.11.cloned.1.call-done = f32[4,256,256]{2,1,0:T(8,128)} async-done(((f32[1,256,256]{2,1,0:T(8,128)}), f32[4,256,256]{2,1,0:T(8,128)}) %all-gather.11.cloned.1.call-update) | async-done | bytes 1048592 | tf_op jit(solution)/shard_map/all_gather | solution.py:10
  1179.7 10.3 broadcast_select_fusion.4
  1190.1 288.7 %all-gather.17.cloned.1.call-done = f32[128,256,256]{2,0,1:T(8,128)} async-done(((f32[16,256,256]{2,0,1:T(8,128)}), f32[128,256,256]{2,0,1:T(8,128)}) %all-gather.17.cloned.1.call-update) | async-done | bytes 33554448 | tf_op jit(solution)/shard_map/all_gather | solution.py:10
  1478.8 15.4 reduce_sum.56
  1503.2 24.5 %all-gather.13.cloned.1.call-done = f32[4,256,256]{2,1,0:T(8,128)} async-done(((f32[1,256,256]{2,1,0:T(8,128)}), f32[4,256,256]{2,1,0:T(8,128)}) %all-gather.13.cloned.1.call-update) | async-done | bytes 1048592 | tf_op jit(solution)/shard_map/all_gather | solution.py:10
  1529.0 8.9 fusion.9
  1538.0 288.7 %all-gather.19.cloned.1.call-done = f32[128,256,256]{2,0,1:T(8,128)} async-done(((f32[16,256,256]{2,0,1:T(8,128)}), f32[128,256,256]{2,0,1:T(8,128)}) %all-gather.19.cloned.1.call-update) | async-done | bytes 33554448 | tf_op jit(solution)/shard_map/all_gather | solution.py:10
  1826.7 15.3 reduce_sum.58
  1854.3 15.1 reshape.334
  1869.4 10.1 broadcast_select_fusion
  1887.5 218.1 %all-gather.21.cloned.1.call-done = f32[32,1,256,768]{3,1,0,2:T(1,128)} async-done(((f32[8,1,256,768]{3,1,0,2:T(1,128)}), f32[32,1,256,768]{3,1,0,2:T(1,128)}) %all-gather.21.cloned.1.call-update) | async-done | bytes 25165840 | tf_op jit(solution)/shard_map/all_gather | solution.py:10
  2105.6 20.7 bitcast_reduce_fusion
  2126.3 87.7 %fusion.5 = f32[16,256,8,256]{3,0,2,1:T(8,128)} fusion(f32[8,256,768]{2,0,1:T(8,128)} %bitcast_reduce_fusion, f32[16,256,256]{2,0,1:T(8,128)} %copy-done.9, f32[16,256,256]{2,0,1:T(8,128)S(1)} %copy-done.5, f32[16,256,256]{2,0,1:T(8,128)S(1)} %copy-done.8), kind=kOutput, calls=%fused_computation.17 | convolution fusion | flops 77315702784 | bytes 52428800 | tf_op jit(solution)/shard_map/axk,byk->axby/dot_general | solution.py:88
  2214.0 38.1 %subtract_select_fusion = f32[16,256,8,256]{3,2,0,1:T(8,128)} fusion(f32[16,256,8,256]{3,2,0,1:T(8,128)} %bitcast_add_fusion, f32[16,256,8,256]{3,0,2,1:T(8,128)} %fusion.5, pred[16,8]{1,0:T(8,128)(4,1)S(1)} %copy.144), kind=kLoop, calls=%fused_computation.8 | loop fusion | flops 16777216 | bytes 100663424 | tf_op jit(solution)/shard_map/jit(_where)/select_n | solution.py:97
  2252.1 15.2 broadcast_select_fusion.2
  2267.3 90.7 %scatter.4 = f32[16,256,8,256]{3,2,0,1:T(8,128)} dynamic-update-slice(f32[16,256,8,256]{3,2,0,1:T(8,128)} %subtract_select_fusion, f32[16,256,1,256]{3,2,0,1:T(1,128)} %broadcast_select_fusion.2, s32[]{:T(128)} %constant.196.clone.1, s32[]{:T(128)} %constant.196.clone.1, s32[]{:T(128)} %constant.196.clone.1, s32[]{:T(128)} %constant.196.clone.1) | dynamic-update-slice | bytes 8388612 | tf_op jit(solution)/shard_map/scatter | solution.py:103
  2358.0 22.9 copy.178
  (101 shorter events, 59.8 us)
Async XLA Ops:
  6.5 257.3 %copy-start = (s32[8]{0:T(128)S(1)}, s32[8]{0:T(128)}, u32[]{:S(2)}) copy-start(s32[8]{0:T(128)} %param.11) | copy-start | bytes 100
  38.4 190.7 %all-to-all-start = ((f32[2,4,4,256,512]{4,3,2,0,1:T(8,128)}), f32[2,4,4,256,512]{4,3,2,0,1:T(8,128)}, u32[]{:S(2)}, u32[]{:S(2)}) async-start(f32[2,4,4,256,512]{4,3,2,0,1:T(8,128)} %copy.152), calls=%async_computation | async-start | bytes 33554432 | tf_op jit(solution)/shard_map/all_to_all | solution.py:46
  255.6 6.8 copy-start.2
  255.6 369.6 %all-to-all-start.1 = ((f32[8,1,4,256,512]{4,3,2,1,0:T(8,128)}), f32[8,1,4,256,512]{4,3,2,1,0:T(8,128)}, u32[]{:S(2)}, u32[]{:S(2)}) async-start(f32[8,1,4,256,512]{4,3,2,1,0:T(8,128)} %fusion.2), calls=%async_computation.1 | async-start | bytes 33554432 | tf_op jit(solution)/shard_map/all_to_all | solution.py:54
  261.5 843.1 %all-gather.15.cloned.1.call-start = ((), (), s32[]{:S(2)}) async-start(), calls=%async_computation.4 | async-start | bytes 37748736 | tf_op jit(solution)/shard_map/all_gather | solution.py:10
  817.9 360.4 %all-gather.11.cloned.1.call-start = ((), (), s32[]{:S(2)}) async-start(), calls=%async_computation.2 | async-start | bytes 1310720 | tf_op jit(solution)/shard_map/all_gather | solution.py:10
  1129.8 15.2 copy-start.10
  1150.4 2.0 copy-start.6
  1153.4 325.4 %all-gather.17.cloned.1.call-start = ((), (), s32[]{:S(2)}) async-start(), calls=%async_computation.5 | async-start | bytes 37748736 | tf_op jit(solution)/shard_map/all_gather | solution.py:10
  1190.0 337.7 %all-gather.13.cloned.1.call-start = ((), (), s32[]{:S(2)}) async-start(), calls=%async_computation.3 | async-start | bytes 1310720 | tf_op jit(solution)/shard_map/all_gather | solution.py:10
  1499.6 2.1 copy-start.3
  1502.7 324.0 %all-gather.19.cloned.1.call-start = ((), (), s32[]{:S(2)}) async-start(), calls=%async_computation.6 | async-start | bytes 37748736 | tf_op jit(solution)/shard_map/all_gather | solution.py:10
  1537.9 567.7 %all-gather.21.cloned.1.call-start = ((), (), s32[]{:S(2)}) async-start(), calls=%async_computation.7 | async-start | bytes 31457280 | tf_op jit(solution)/shard_map/all_gather | solution.py:10
  1842.0 7.5 copy-start.4
  1842.0 7.5 copy-start.7
  1847.6 1.9 copy-start.9
  1879.5 0.8 copy-start.11
  2105.6 20.7 copy-start.5
  2105.6 20.7 copy-start.8
  2358.0 22.9 copy-start.1
Sparse Core Ops, SparseCore 0:
  818.1 286.5 all-gather.14
  1153.5 24.8 all-gather.10
  1190.1 288.6 all-gather.16
  1502.8 24.8 all-gather.12
  1538.0 288.6 all-gather.18
  1879.7 225.8 all-gather.20
